TPU v7x, 32 devices: a whole 2x2x4 slice. The times are simulated.
32 devices in a mesh: grp: 4 (over y, x), peer: 8 (over z, core).
Axes of the slice: x: 2, y: 2, z: 4, core: 2. Of those that a mesh axis runs over, the one named last changes fastest.
Arguments:
- embeddings: bfloat16 [16384, 768], P(('grp', 'peer')), may hold values from -6 to 6
- seed_labels: float32 [16384, 128], P(('grp', 'peer')), may hold values from -6 to 6
- cluster_ids: int32 [16384], P(('grp', 'peer')), may hold values from 0 to 63, as said below
- owner_map: int32 [64], replicated, may hold values from 0 to 31, as said below
- seed_flags: int32 [16384], P(('grp', 'peer')), may hold values 0 or 1
Outputs:
- refined: float32 [16384, 128], P(('grp', 'peer'))
Inputs may be any that keep to these rules, and one draw needn't show every extreme that they name: `cluster_ids`: within each device's aligned block of 512 rows, at most 32 rows name clusters owned by any one device; one device owns clusters named by exactly 32 rows of every block. `owner_map`: every device owns exactly 2 clusters.
All inputs are finite; a program needn't handle non-finite values. No bound on the sum of `seed_flags` on one device may be relied on, other than what follows from the above.
Results may differ from a plain program's by a relative error of at most 0.0031.
Values may be sent and summed in bfloat16 or wider, within the bound.
A program may use at most 64 MiB of HBM per device.

v0:
```python
import math

import jax
import jax.numpy as jnp
from jax import lax
from jax.sharding import PartitionSpec as P

STEPS = 3


label_mix = 0.8
cross_penalty = 2.0


def affinity_rows(queries, keys, query_clusters, key_clusters, key_valid, offset):
    scale = 2.0 / math.sqrt(keys.shape[1])
    scores = (
        lax.dot_general(queries, keys, (((1,), (1,)), ((), ())), preferred_element_type=jnp.float32)
        * scale
    )
    query_pos = offset + jnp.arange(queries.shape[0], dtype=jnp.int32)
    key_pos = jnp.arange(keys.shape[0], dtype=jnp.int32)
    differ = query_clusters[:, None] != key_clusters[None, :]
    scores = jnp.where(differ, scores - cross_penalty, scores)
    scores = jnp.where(key_valid[None, :], scores, -jnp.inf)
    scores = jnp.where(query_pos[:, None] == key_pos[None, :], 0.0, scores)
    highest = jnp.max(scores, axis=1, keepdims=True)
    weights = jnp.exp(scores - highest)
    return (weights / jnp.sum(weights, axis=1, keepdims=True)).astype(jnp.bfloat16)


def on_device(embeddings, seed_labels, cluster_ids, owner_map, seed_flags):
    row_count = embeddings.shape[0]
    device_count = lax.axis_size(("grp", "peer"))
    slot_count = 2 * row_count
    capacity = slot_count // device_count
    cluster_count = owner_map.shape[0]
    matches = cluster_ids[:, None] == jnp.arange(cluster_count, dtype=jnp.int32)[None, :]
    owner_of = jnp.sum(jnp.where(matches, owner_map[None, :], 0), axis=1)
    member = owner_of[:, None] == jnp.arange(device_count, dtype=jnp.int32)[None, :]
    running = jnp.cumsum(member.astype(jnp.int32), axis=0)
    position = jnp.sum(jnp.where(member, running, 0), axis=1) - 1
    target = owner_of * capacity + position
    source_row = (
        jnp.full((slot_count,), row_count, jnp.int32)
        .at[target]
        .set(jnp.arange(row_count, dtype=jnp.int32))
    )
    send_emb = jnp.take(embeddings, source_row, axis=0, mode="fill", fill_value=0)
    send_lab = jnp.take(seed_labels, source_row, axis=0, mode="fill", fill_value=0)
    side_info = jnp.stack([cluster_ids.astype(jnp.float32), seed_flags.astype(jnp.float32)], axis=1)
    send_info = jnp.take(side_info, source_row, axis=0, mode="fill", fill_value=-1.0)
    got_emb = lax.all_to_all(send_emb, ("grp", "peer"), split_axis=0, concat_axis=0, tiled=True)
    got_lab, got_info = (
        lax.all_to_all(send_lab, ("grp", "peer"), split_axis=0, concat_axis=0, tiled=True),
        lax.all_to_all(send_info, ("grp", "peer"), split_axis=0, concat_axis=0, tiled=True),
    )
    got_clusters = got_info[:, 0].astype(jnp.int32)
    got_seed = got_info[:, 1] > 0.5
    got_valid = got_clusters >= 0
    block = min(512, slot_count)
    pieces = []
    for offset in range(0, slot_count, block):
        pieces.append(
            affinity_rows(
                got_emb[offset : offset + block],
                got_emb,
                got_clusters[offset : offset + block],
                got_clusters,
                got_valid,
                offset,
            )
        )
    affinity = jnp.concatenate(pieces, axis=0)
    current = got_lab
    for sweep in range(STEPS):
        spread = jnp.dot(affinity, current.astype(jnp.bfloat16), preferred_element_type=jnp.float32)
        current = jnp.where(
            got_seed[:, None], got_lab, label_mix * spread + (1.0 - label_mix) * got_lab
        )
    returned = lax.all_to_all(current, ("grp", "peer"), split_axis=0, concat_axis=0, tiled=True)
    return jnp.take(returned, target, axis=0)


def solution(mesh):
    in_specs = (
        P(("grp", "peer"), None),
        P(("grp", "peer"), None),
        P(("grp", "peer")),
        P(),
        P(("grp", "peer")),
    )
    out_specs = P(("grp", "peer"), None)
    return jax.shard_map(
        on_device, mesh=mesh, in_specs=in_specs, out_specs=out_specs, check_vma=False
    )
```

profile of v0, /device:TPU:0, one launch (start us, length us, event | category | flops | bytes accessed | tf_op | source)
XLA Modules:
  0.0 112.9 jit_solution(16370897008557589524)
XLA Ops:
  0.0 0.8 convert_element_type.40
  0.8 0.8 select_reduce_fusion
  1.6 1.2 %reduce-window.6 = s32[32,4,128]{2,0,1:T(8,128)S(1)} reduce-window(s32[32,4,128]{2,0,1:T(8,128)S(1)} %fusion.22, s32[]{:T(128)} %constant.42.clone.1), window={size=1x1x128 pad=0_0x0_0x127_0}, to_apply=%region_1.2 | reduce-window | flops 2080768 | bytes 131076 | tf_op jit(solution)/shard_map/reduce-window
  3.1 2.4 %scatter_custom_fusion = s32[1024]{0:T(1024)S(1)} fusion(s32[512]{0:T(512)S(1)} %bitcast.54, s32[512]{0:T(512)S(1)} %iota.29, s32[]{:T(128)} %constant.53.clone.1), kind=kCustom, calls=%fused_computation.61 | custom fusion | bytes 4100 | tf_op jit(solution)/shard_map/scatter | solution.py:47
  6.5 2.8 %gather_fusion = f32[1024,2]{1,0:T(8,128)S(1)} fusion(f32[512,2]{1,0:T(8,128)S(1)} %copy.18, s32[1024]{0:T(1024)S(1)} %fusion.23), kind=kCustom, calls=%fused_computation | custom fusion | bytes 20480 | tf_op jit(solution)/shard_map/jit(_take)/gather | solution.py:52
  10.3 7.3 %all-to-all-start = ((f32[32,32,2]{1,2,0:T(2,128)}), f32[32,32,2]{1,2,0:T(2,128)S(1)}, u32[]{:S(2)}, u32[]{:S(2)}) async-start(f32[32,32,2]{1,2,0:T(2,128)} %broadcast_select_fusion.3), calls=%async_computation | async-start | bytes 65536 | tf_op jit(solution)/shard_map/all_to_all | solution.py:56
  17.6 4.0 %gather_fusion.2 = bf16[1024,768]{1,0:T(8,128)(2,1)S(1)} fusion(bf16[512,768]{1,0:T(8,128)(2,1)S(1)} %copy-done, s32[1024]{0:T(1024)S(1)} %fusion.23), kind=kCustom, calls=%fused_computation.2 | custom fusion | bytes 3149824 | tf_op jit(solution)/shard_map/jit(_take)/gather | solution.py:49
  21.6 1.4 %broadcast_select_fusion = bf16[32,32,768]{2,1,0:T(8,128)(2,1)} fusion(bf16[32,32,768]{2,1,0:T(8,128)(2,1)S(1)} %bitcast.42, pred[32,32]{1,0:T(8,128)(4,1)S(1)} %broadcast_in_dim.128), kind=kLoop, calls=%fused_computation.20 | loop fusion | flops 786432 | bytes 3146752 | tf_op jit(solution)/shard_map/jit(_take)/select_n | solution.py:49
  23.0 1.9 %all-to-all-done = f32[32,32,2]{1,2,0:T(2,128)S(1)} async-done(((f32[32,32,2]{1,2,0:T(2,128)}), f32[32,32,2]{1,2,0:T(2,128)S(1)}, u32[]{:S(2)}, u32[]{:S(2)}) %all-to-all-start) | async-done | bytes 8224 | tf_op jit(solution)/shard_map/all_to_all | solution.py:56
  24.8 4.0 %all-to-all-start.2 = ((bf16[32,32,768]{2,1,0:T(8,128)(2,1)}), bf16[32,32,768]{2,1,0:T(8,128)(2,1)S(1)}, u32[]{:S(2)}, u32[]{:S(2)}) async-start(bf16[32,32,768]{2,1,0:T(8,128)(2,1)} %broadcast_select_fusion), calls=%async_computation.2 | async-start | bytes 3145728 | tf_op jit(solution)/shard_map/all_to_all | solution.py:53
  28.8 2.8 %gather_fusion.1 = f32[1024,128]{1,0:T(8,128)S(1)} fusion(f32[512,128]{1,0:T(8,128)S(1)} %copy-done.1, s32[1024]{0:T(1024)S(1)} %fusion.23), kind=kCustom, calls=%fused_computation.1 | custom fusion | bytes 1052672 | tf_op jit(solution)/shard_map/jit(_take)/gather | solution.py:50
  31.7 1.0 broadcast_select_fusion.1
  32.8 34.9 %all-to-all-done.2 = bf16[32,32,768]{2,1,0:T(8,128)(2,1)S(1)} async-done(((bf16[32,32,768]{2,1,0:T(8,128)(2,1)}), bf16[32,32,768]{2,1,0:T(8,128)(2,1)S(1)}, u32[]{:S(2)}, u32[]{:S(2)}) %all-to-all-start.2) | async-done | bytes 1572896 | tf_op jit(solution)/shard_map/all_to_all | solution.py:53
  67.7 2.6 %all-to-all-start.1 = ((f32[32,32,128]{2,1,0:T(8,128)}), f32[32,32,128]{2,1,0:T(8,128)S(1)}, u32[]{:S(2)}, u32[]{:S(2)}) async-start(f32[32,32,128]{2,1,0:T(8,128)} %broadcast_select_fusion.1), calls=%async_computation.1 | async-start | bytes 1048576 | tf_op jit(solution)/shard_map/all_to_all | solution.py:55
  70.4 1.3 %fusion.34 = (f32[512]{0:T(512)S(1)}, f32[512,1024]{1,0:T(8,128)S(1)}) fusion(bf16[512,768]{1,0:T(8,128)(2,1)S(1)} %bitcast.46, bf16[1024,768]{1,0:T(8,128)(2,1)S(1)} %bitcast.40, s32[1024]{0:T(1024)S(1)} %bitcast.51, s32[512]{0:T(512)S(1)} %bitcast.60, pred[1024]{0:T(1024)(128)(4,1)S(1)} %broadcast_compare_fusion), kind=kOutput, calls=%fused_computation.72 | convolution fusion | flops 809500160 | bytes 4465664 | tf_op jit(solution)/shard_map/dot_general | solution.py:18
  71.7 1.4 %fusion.33 = (f32[512]{0:T(512)S(1)}, f32[512,1024]{1,0:T(8,128)S(1)}) fusion(bf16[512,768]{1,0:T(8,128)(2,1)S(1)} %bitcast.45, bf16[1024,768]{1,0:T(8,128)(2,1)S(1)} %bitcast.41, s32[1024]{0:T(1024)S(1)} %bitcast.52, s32[512]{0:T(512)S(1)} %bitcast.59, pred[1024]{0:T(1024)(128)(4,1)S(1)} %broadcast_compare_fusion, s32[512]{0:T(512)S(1)} %iota_add_fusion), kind=kOutput, calls=%fused_computation.71 | convolution fusion | flops 809500160 | bytes 4467712 | tf_op jit(solution)/shard_map/dot_general | solution.py:18
  74.1 0.7 divide_convert_fusion
  74.9 11.8 %all-to-all-done.1 = f32[32,32,128]{2,1,0:T(8,128)S(1)} async-done(((f32[32,32,128]{2,1,0:T(8,128)}), f32[32,32,128]{2,1,0:T(8,128)S(1)}, u32[]{:S(2)}, u32[]{:S(2)}) %all-to-all-start.1) | async-done | bytes 524320 | tf_op jit(solution)/shard_map/all_to_all | solution.py:55
  86.7 2.9 %fusion.13 = bf16[1024,128]{1,0:T(8,128)(2,1)} fusion(f32[1024,128]{1,0:T(8,128)S(1)} %bitcast.47, bf16[512,1024]{1,0:T(8,128)(2,1)S(1)} %get-tuple-element.15, bf16[512,1024]{1,0:T(8,128)(2,1)S(1)} %get-tuple-element.16, pred[1024]{0:T(1024)(128)(4,1)S(1)} %compare_reduce_fusion), kind=kOutput, calls=%fused_computation.31 | convolution fusion | flops 546701312 | bytes 2884608 | tf_op jit(solution)/shard_map/dot_general | solution.py:77
  89.6 2.4 %fusion.7 = f32[1024,128]{1,0:T(8,128)} fusion(f32[1024,128]{1,0:T(8,128)S(1)} %bitcast.48, bf16[1024,128]{1,0:T(8,128)(2,1)} %fusion.13, bf16[512,1024]{1,0:T(8,128)(2,1)S(1)} %get-tuple-element.15, bf16[512,1024]{1,0:T(8,128)(2,1)S(1)} %get-tuple-element.16, pred[1024]{0:T(1024)(128)(4,1)S(1)} %compare_reduce_fusion), kind=kOutput, calls=%fused_computation.23 | convolution fusion | flops 273154048 | bytes 3408896 | tf_op jit(solution)/shard_map/dot_general | solution.py:77
  92.0 2.6 %all-to-all-start.3 = ((f32[32,32,128]{2,1,0:T(8,128)}), f32[32,32,128]{2,1,0:T(8,128)S(1)}, u32[]{:S(2)}, u32[]{:S(2)}) async-start(f32[32,32,128]{2,1,0:T(8,128)} %bitcast.49), calls=%async_computation.3 | async-start | bytes 1048576 | tf_op jit(solution)/shard_map/all_to_all | solution.py:81
  94.7 16.3 %all-to-all-done.3 = f32[32,32,128]{2,1,0:T(8,128)S(1)} async-done(((f32[32,32,128]{2,1,0:T(8,128)}), f32[32,32,128]{2,1,0:T(8,128)S(1)}, u32[]{:S(2)}, u32[]{:S(2)}) %all-to-all-start.3) | async-done | bytes 524320 | tf_op jit(solution)/shard_map/all_to_all | solution.py:81
  111.0 1.0 gather_fusion.3
  112.0 0.8 broadcast_select_fusion.2
  (31 shorter events, 3.5 us)
Async XLA Ops:
  0.0 17.6 %copy-start = (bf16[512,768]{1,0:T(8,128)(2,1)S(1)}, bf16[512,768]{1,0:T(8,128)(2,1)}, u32[]{:S(2)}) copy-start(bf16[512,768]{1,0:T(8,128)(2,1)} %param.5) | copy-start | bytes 2359300
  10.3 14.5 %all-to-all-start = ((f32[32,32,2]{1,2,0:T(2,128)}), f32[32,32,2]{1,2,0:T(2,128)S(1)}, u32[]{:S(2)}, u32[]{:S(2)}) async-start(f32[32,32,2]{1,2,0:T(2,128)} %broadcast_select_fusion.3), calls=%async_computation | async-start | bytes 65536 | tf_op jit(solution)/shard_map/all_to_all | solution.py:56
  23.0 5.8 %copy-start.1 = (f32[512,128]{1,0:T(8,128)S(1)}, f32[512,128]{1,0:T(8,128)}, u32[]{:S(2)}) copy-start(f32[512,128]{1,0:T(8,128)} %param.6) | copy-start | bytes 786436
  24.8 42.9 %all-to-all-start.2 = ((bf16[32,32,768]{2,1,0:T(8,128)(2,1)}), bf16[32,32,768]{2,1,0:T(8,128)(2,1)S(1)}, u32[]{:S(2)}, u32[]{:S(2)}) async-start(bf16[32,32,768]{2,1,0:T(8,128)(2,1)} %broadcast_select_fusion), calls=%async_computation.2 | async-start | bytes 3145728 | tf_op jit(solution)/shard_map/all_to_all | solution.py:53
  67.7 19.0 %all-to-all-start.1 = ((f32[32,32,128]{2,1,0:T(8,128)}), f32[32,32,128]{2,1,0:T(8,128)S(1)}, u32[]{:S(2)}, u32[]{:S(2)}) async-start(f32[32,32,128]{2,1,0:T(8,128)} %broadcast_select_fusion.1), calls=%async_computation.1 | async-start | bytes 1048576 | tf_op jit(solution)/shard_map/all_to_all | solution.py:55
  92.0 19.0 %all-to-all-start.3 = ((f32[32,32,128]{2,1,0:T(8,128)}), f32[32,32,128]{2,1,0:T(8,128)S(1)}, u32[]{:S(2)}, u32[]{:S(2)}) async-start(f32[32,32,128]{2,1,0:T(8,128)} %bitcast.49), calls=%async_computation.3 | async-start | bytes 1048576 | tf_op jit(solution)/shard_map/all_to_all | solution.py:81
where the time goes:
time: 113 us
  waiting for transfers between devices  64.8 us (57%)
  starting transfers between devices  16.5 us (15%)
  local copies, waits for them, and re-layouts  14 us (12%)
  other arithmetic  9.28 us (8%)
  matrix products  8.06 us (7%)
    all_to_all x1, waiting for transfers between devices, on_device(): lax.all_to_all(send_emb, ('grp', 'peer'), split_axis=0, concat_axis=0, ti...  34.9 us
    all_to_all x1, waiting for transfers between devices, on_device(): lax.all_to_all(current, ('grp', 'peer'), split_axis=0, concat_axis=0, til...  16.3 us
    all_to_all x1, waiting for transfers between devices, on_device(): lax.all_to_all(send_lab, ('grp', 'peer'), split_axis=0, concat_axis=0, ti...  11.8 us
    all_to_all x1, starting transfers between devices, on_device(): lax.all_to_all(send_info, ('grp', 'peer'), split_axis=0, concat_axis=0, t...  7.3 us
    dot_general x2, matrix products, on_device(): jnp.dot(affinity, current.astype(jnp.bfloat16), preferred_element_type=jn...  5.38 us
    gather x1, local copies, waits for them, and re-layouts, on_device(): jnp.take(embeddings, source_row, axis=0, mode='fill', fill_value=0)  4 us
    all_to_all x1, starting transfers between devices, on_device(): lax.all_to_all(send_emb, ('grp', 'peer'), split_axis=0, concat_axis=0, ti...  3.98 us
    gather x2, local copies, waits for them, and re-layouts, on_device(): jnp.take(side_info, source_row, axis=0, mode='fill', fill_value=-1.0)  3.07 us
  transfers between devices with their start and end apart: 4, of which 4 were waited for; matrix products, arithmetic and copies ran while one was open for 12% of the time, Pallas kernels for 0%

commit v1 on v0

v1 whole, which is shorter than its diff:
```python
import functools
import math

import jax
import jax.numpy as jnp
from jax import lax
from jax.experimental import pallas as pl
from jax.experimental.pallas import tpu as pltpu
from jax.sharding import PartitionSpec as P

STEPS = 3
label_mix = 0.8
cross_penalty = 2.0
MESH = pl.DeviceIdType.MESH
EMB, LABEL, INFO, BACK = range(4)
HALF = 64
NT = (((1,), (1,)), ((), ()))


def dot(a, b):
    return jnp.dot(a, b, preferred_element_type=jnp.float32)


def dot_nt(a, b):
    return lax.dot_general(a, b, NT, preferred_element_type=jnp.float32)


def iota(shape, dim):
    return lax.broadcasted_iota(jnp.int32, shape, dim)


def one_hot(mask):
    return jnp.where(mask, 1.0, 0.0).astype(jnp.bfloat16)


def kernel(
    n_grp, n_peer, cap,
    emb_ref, lab_ref, ids_ref, own_ref, flg_ref, out_ref,
    send_emb, send_lab, send_info, recv_emb, recv_lab, recv_info, send_back, recv_back,
    target_row, affinity, carried, send_sem, recv_sem,
):
    n = n_grp * n_peer
    my_grp, my_peer = lax.axis_index("grp"), lax.axis_index("peer")
    me = my_grp * n_peer + my_peer
    rows, slots = emb_ref.shape[0], n * cap
    chunk = n_peer * cap

    def block(device):
        return pl.ds(pl.multiple_of(device * cap, cap), cap)

    def part(kind, device):
        return {
            EMB: (send_emb.at[block(device), :], recv_emb),
            LABEL: (send_lab.at[block(device), :], recv_lab),
            BACK: (send_back.at[block(device), :], recv_back),
        }[kind]

    def copy(kind, device, source):
        if kind == INFO:
            src, dst = send_info.at[device], recv_info.at[source]
        else:
            src, buffer = part(kind, device)
            dst = buffer.at[block(source), :]
        return pltpu.make_async_remote_copy(
            src_ref=src,
            dst_ref=dst,
            send_sem=send_sem.at[kind, device],
            recv_sem=recv_sem.at[kind, source],
            device_id=(device // n_peer, lax.rem(device, n_peer)),
            device_id_type=MESH,
        )

    def others(body):
        def one(k, _):
            body(lax.rem(me + k, n))
            return 0

        lax.fori_loop(1, n, one, 0)

    barrier = pltpu.get_barrier_semaphore()
    others(
        lambda d: pl.semaphore_signal(
            barrier, inc=1, device_id=(d // n_peer, lax.rem(d, n_peer)), device_id_type=MESH
        )
    )

    ids = ids_ref[...].reshape(1, rows)
    flags = flg_ref[...].reshape(1, rows)
    clusters = own_ref.shape[0]
    owners = own_ref[...].reshape(1, clusters).astype(jnp.bfloat16)
    owners = jnp.broadcast_to(owners, (16, clusters))
    owner = dot(owners, one_hot(iota((clusters, rows), 0) == ids))[0:1, :].astype(jnp.int32)
    member = iota((n, rows), 0) == owner
    members = one_hot(member)
    running = dot(members, one_hot(iota((rows, rows), 0) <= iota((rows, rows), 1)))
    position = jnp.sum(jnp.where(member, running, 0.0), axis=0, keepdims=True).astype(jnp.int32) - 1
    target = owner * cap + position
    target_row[...] = target
    lane = iota((128, rows), 0)
    entry = jnp.where(
        lane < HALF,
        jnp.where(lane == position, (ids + 1).astype(jnp.float32), 0.0),
        jnp.where(lane - HALF == position, flags.astype(jnp.float32), 0.0),
    ).astype(jnp.bfloat16)
    send_info[...] = dot_nt(members, entry).reshape(n, 1, 128)
    recv_info[me] = send_info[me]

    pl.semaphore_wait(barrier, n - 1)

    def send_chunk(j, _):
        g = lax.rem(my_grp + j, n_grp)
        start = pl.multiple_of(g * chunk, chunk)
        pick = one_hot(iota((chunk, rows), 0) + start == target_row[...])
        send_emb[pl.ds(start, chunk), :] = dot(pick, emb_ref[...]).astype(jnp.bfloat16)

        def one(k, _):
            d = g * n_peer + lax.rem(my_peer + k, n_peer)

            @pl.when(d != me)
            def _():
                copy(EMB, d, me).start()

            return 0

        lax.fori_loop(0, n_peer, one, 0)
        send_lab[pl.ds(start, chunk), :] = dot(pick, lab_ref[...].astype(jnp.bfloat16)).astype(jnp.bfloat16)
        return 0

    lax.fori_loop(1, n_grp + 1, send_chunk, 0)

    def send_small(d):
        copy(INFO, d, me).start()
        copy(LABEL, d, me).start()

    others(send_small)
    recv_emb[block(me), :] = send_emb[block(me), :]
    recv_lab[block(me), :] = send_lab[block(me), :]

    others(lambda s: copy(EMB, s, s).wait_recv())
    others(lambda s: copy(INFO, s, s).wait_recv())

    info = recv_info[...].reshape(n, 128).astype(jnp.bfloat16)
    slot = iota((slots, 128), 0)
    place = iota((slots, 128), 1)
    spread_info = dot(one_hot(iota((slots, n), 0) // cap == iota((slots, n), 1)), info)
    here = slot - slot // cap * cap
    cluster_col = jnp.sum(jnp.where(place == here, spread_info, 0.0), axis=1, keepdims=True)
    seed_col = jnp.sum(jnp.where(place == here + HALF, spread_info, 0.0), axis=1, keepdims=True)
    along = iota((128, slots), 1)
    wide = dot(info, one_hot(iota((128, slots), 0) == along - along // cap * cap))
    cluster_row = jnp.sum(
        jnp.where(iota((n, slots), 0) == iota((n, slots), 1) // cap, wide, 0.0), axis=0, keepdims=True
    )
    scale = 2.0 / math.sqrt(emb_ref.shape[1])
    for offset in range(0, slots, chunk):
        score = dot_nt(recv_emb[pl.ds(offset, chunk), :], recv_emb[...]) * scale
        score = jnp.where(cluster_col[offset : offset + chunk] != cluster_row, score - cross_penalty, score)
        score = jnp.where(cluster_row > 0.5, score, -1e30)
        score = jnp.where(iota(score.shape, 0) + offset == iota(score.shape, 1), 0.0, score)
        weight = jnp.exp(score - jnp.max(score, axis=1, keepdims=True))
        total = jnp.sum(weight, axis=1, keepdims=True)
        affinity[pl.ds(offset, chunk), :] = (weight * (1.0 / total)).astype(jnp.bfloat16)

    others(lambda s: copy(LABEL, s, s).wait_recv())
    given = recv_lab[...].astype(jnp.float32)
    fixed = seed_col > 0.5
    carried[...] = recv_lab[...]
    for sweep in range(STEPS - 1):
        spread = dot(affinity[...], carried[...])
        current = jnp.where(fixed, given, label_mix * spread + (1.0 - label_mix) * given)
        carried[...] = current.astype(jnp.bfloat16)

    def back_chunk(j, _):
        g = lax.rem(my_grp + j, n_grp)
        piece = pl.ds(pl.multiple_of(g * chunk, chunk), chunk)
        send_back[piece, :] = dot(affinity[piece, :], carried[...]).astype(jnp.bfloat16)

        def one(k, _):
            d = g * n_peer + lax.rem(my_peer + k, n_peer)

            @pl.when(d != me)
            def _():
                copy(BACK, d, me).start()

            return 0

        lax.fori_loop(0, n_peer, one, 0)
        return 0

    lax.fori_loop(1, n_grp + 1, back_chunk, 0)
    recv_back[block(me), :] = send_back[block(me), :]

    side = jnp.concatenate([target_row[...], flags, jnp.zeros((6, rows), jnp.int32)], axis=0)
    side = jnp.transpose(side.astype(jnp.float32)).astype(jnp.int32)
    home = one_hot(iota((rows, slots), 1) == side[:, 0:1])
    kept = side[:, 1:2] > 0
    others(lambda s: copy(BACK, s, s).wait_recv())
    spread = dot(home, recv_back[...])
    seed = lab_ref[...]
    out_ref[...] = jnp.where(kept, seed, label_mix * spread + (1.0 - label_mix) * seed)

    def sent(d):
        for kind in (EMB, LABEL, INFO, BACK):
            copy(kind, d, me).wait_send()

    others(sent)


def solution(mesh):
    n_grp, n_peer = mesh.shape["grp"], mesh.shape["peer"]
    n = n_grp * n_peer

    def step(embeddings, seed_labels, cluster_ids, owner_map, seed_flags):
        rows, depth = embeddings.shape
        width = seed_labels.shape[1]
        cap = max(2 * rows // n, 16)
        slots = n * cap
        buffers = [
            pltpu.VMEM((slots, depth), jnp.bfloat16),
            pltpu.VMEM((slots, width), jnp.bfloat16),
            pltpu.VMEM((n, 1, 128), jnp.float32),
        ]
        return pl.pallas_call(
            functools.partial(kernel, n_grp, n_peer, cap),
            out_shape=jax.ShapeDtypeStruct((rows, width), jnp.float32),
            in_specs=[pl.BlockSpec(memory_space=pltpu.VMEM)] * 5,
            out_specs=pl.BlockSpec(memory_space=pltpu.VMEM),
            scratch_shapes=[
                *buffers,
                *buffers,
                pltpu.VMEM((slots, width), jnp.bfloat16),
                pltpu.VMEM((slots, width), jnp.bfloat16),
                pltpu.VMEM((1, rows), jnp.int32),
                pltpu.VMEM((slots, slots), jnp.bfloat16),
                pltpu.VMEM((slots, width), jnp.bfloat16),
                pltpu.SemaphoreType.DMA((4, n)),
                pltpu.SemaphoreType.DMA((4, n)),
            ],
            compiler_params=pltpu.CompilerParams(
                collective_id=0, has_side_effects=True, vmem_limit_bytes=56 * 1024 * 1024
            ),
        )(embeddings, seed_labels, cluster_ids, owner_map, seed_flags)

    rows = P(("grp", "peer"))
    return jax.shard_map(
        step,
        mesh=mesh,
        in_specs=(P(("grp", "peer"), None), P(("grp", "peer"), None), rows, P(), rows),
        out_specs=P(("grp", "peer"), None),
        check_vma=False,
    )
```

time: 113 us -> 70.9 us (0.63)
  Pallas kernels: 0 us -> 69 us
  waiting for transfers between devices: 64.8 us -> 0 us
  starting transfers between devices: 16.5 us -> 0 us
  local copies, waits for them, and re-layouts: 14 us -> 1.67 us
  other arithmetic: 9.28 us -> 0 us
  matrix products: 8.06 us -> 0 us
    pallas_call x0 -> x1, Pallas kernels: none -> 69 us  [step(): pl.pallas_call(functools.partial(kernel, n_grp, n_peer, cap), out_shape=j...]
    all_to_all x4 -> x0, waiting for transfers between devices: 64.8 us -> none  [the longest x1 34.9 us: on_device(): lax.all_to_all(send_emb, ('grp', 'peer'), split_axis=0, concat_axis=0, ti...]
    all_to_all x4 -> x0, starting transfers between devices: 16.5 us -> none  [the longest x1 7.3 us: on_device(): lax.all_to_all(send_info, ('grp', 'peer'), split_axis=0, concat_axis=0, t...]
    gather x5 -> x0, local copies, waits for them, and re-layouts: 10.9 us -> none  [the longest x1 4 us: on_device(): jnp.take(embeddings, source_row, axis=0, mode='fill', fill_value=0)]
    dot_general x4 -> x0, matrix products: 8.06 us -> none  [the longest x2 5.38 us: on_device(): jnp.dot(affinity, current.astype(jnp.bfloat16), preferred_element_type=jn...]
    select_n x5 -> x0, other arithmetic: 3.88 us -> none  [the longest x1 1.36 us: on_device(): jnp.take(embeddings, source_row, axis=0, mode='fill', fill_value=0)]
    scatter x1 -> x0, local copies, waits for them, and re-layouts: 2.45 us -> none  [on_device(): source_row = jnp.full((slot_count,), row_count, jnp.int32).at[target].set...]
    convert_element_type x5 -> x0, other arithmetic: 2.2 us -> none  [the longest x1 0.76 us: on_device(): cluster_ids.astype(jnp.float32)]
  transfers between devices with their start and end apart: 4 -> 0, of which waited for: 4 -> 0; matrix products, arithmetic and copies ran while one was open for 12% -> 0% of each run, Pallas kernels for 0% -> 0%
where the time goes in v1:
time: 70.9 us; the launch traced here: 70.7 us
  Pallas kernels  69 us (97%)
  local copies, waits for them, and re-layouts  1.67 us (2%)
    pallas_call x1, Pallas kernels, step(): pl.pallas_call(functools.partial(kernel, n_grp, n_peer, cap), out_shape=j...  69 us
    unnamed x1, local copies, waits for them, and re-layouts  1.67 us

profile of v1, /device:TPU:0, one launch (start us, length us, event | category | flops | bytes accessed | tf_op | source)
XLA Modules:
  0.0 70.7 jit_solution(9060935828940152246)
XLA Ops:
  0.0 69.0 %shard_map.55 = f32[512,128]{1,0:T(8,128)} custom-call(bf16[512,768]{1,0:T(8,128)(2,1)} %emb_ref.1, f32[512,128]{1,0:T(8,128)} %lab_ref.1, s32[512]{0:T(512)} %ids_ref.1, s32[64]{0:T(128)} %own_ref.1, s32[512]{0:T(512)} %flg_ref.1), custom_call_target="tpu_custom_call" | custom-call | tf_op jit(solution)/shard_map/pallas_call | solution.py:223
  69.0 1.7 %copy.7 = f32[512,128]{1,0:T(8,128)} copy(f32[512,128]{1,0:T(8,128)} %shard_map.55) | data formatting | bytes 524288

commit v2 on v1

--- a/solution.py
+++ b/solution.py
@@ -37,7 +37,7 @@
     n_grp, n_peer, cap,
     emb_ref, lab_ref, ids_ref, own_ref, flg_ref, out_ref,
     send_emb, send_lab, send_info, recv_emb, recv_lab, recv_info, send_back, recv_back,
-    target_row, affinity, carried, send_sem, recv_sem,
+    target_row, home, affinity, carried, send_sem, recv_sem,
 ):
     n = n_grp * n_peer
     my_grp, my_peer = lax.axis_index("grp"), lax.axis_index("peer")
@@ -64,23 +64,43 @@
         return pltpu.make_async_remote_copy(
             src_ref=src,
             dst_ref=dst,
-            send_sem=send_sem.at[kind, device],
-            recv_sem=recv_sem.at[kind, source],
-            device_id=(device // n_peer, lax.rem(device, n_peer)),
+            send_sem=send_sem.at[kind],
+            recv_sem=recv_sem.at[kind],
+            device_id=(lax.div(device, n_peer), lax.rem(device, n_peer)),
             device_id_type=MESH,
         )
 
+    def whole(kind):
+        source, landing = {
+            EMB: (send_emb, recv_emb),
+            LABEL: (send_lab, recv_lab),
+            INFO: (send_info, recv_info),
+            BACK: (send_back, recv_back),
+        }[kind]
+        part = pl.ds(0, (n - 1) * (1 if kind == INFO else cap))
+        right = lax.rem(me + 1, n)
+        return pltpu.make_async_remote_copy(
+            src_ref=source.at[part],
+            dst_ref=landing.at[part],
+            send_sem=send_sem.at[kind],
+            recv_sem=recv_sem.at[kind],
+            device_id=(lax.div(right, n_peer), lax.rem(right, n_peer)),
+            device_id_type=MESH,
+        )
+
     def others(body):
-        def one(k, _):
+        for k in range(1, n):
             body(lax.rem(me + k, n))
-            return 0
-
-        lax.fori_loop(1, n, one, 0)
+
+    def members_of(j, body):
+        g = lax.rem(my_grp + j, n_grp)
+        for k in range(1 if j == n_grp else 0, n_peer):
+            body(g * n_peer + lax.rem(my_peer + k, n_peer))
 
     barrier = pltpu.get_barrier_semaphore()
     others(
         lambda d: pl.semaphore_signal(
-            barrier, inc=1, device_id=(d // n_peer, lax.rem(d, n_peer)), device_id_type=MESH
+            barrier, inc=1, device_id=(lax.div(d, n_peer), lax.rem(d, n_peer)), device_id_type=MESH
         )
     )
 
@@ -105,40 +125,27 @@
     send_info[...] = dot_nt(members, entry).reshape(n, 1, 128)
     recv_info[me] = send_info[me]
 
-    pl.semaphore_wait(barrier, n - 1)
-
-    def send_chunk(j, _):
+    for j in range(1, n_grp + 1):
         g = lax.rem(my_grp + j, n_grp)
         start = pl.multiple_of(g * chunk, chunk)
         pick = one_hot(iota((chunk, rows), 0) + start == target_row[...])
         send_emb[pl.ds(start, chunk), :] = dot(pick, emb_ref[...]).astype(jnp.bfloat16)
-
-        def one(k, _):
-            d = g * n_peer + lax.rem(my_peer + k, n_peer)
-
-            @pl.when(d != me)
-            def _():
-                copy(EMB, d, me).start()
-
-            return 0
-
-        lax.fori_loop(0, n_peer, one, 0)
+        if j == 1:
+            pl.semaphore_wait(barrier, n - 1)
+        members_of(j, lambda d: copy(EMB, d, me).start())
+        members_of(j, lambda d: copy(INFO, d, me).start())
         send_lab[pl.ds(start, chunk), :] = dot(pick, lab_ref[...].astype(jnp.bfloat16)).astype(jnp.bfloat16)
-        return 0
-
-    lax.fori_loop(1, n_grp + 1, send_chunk, 0)
-
-    def send_small(d):
-        copy(INFO, d, me).start()
-        copy(LABEL, d, me).start()
-
-    others(send_small)
+
+    others(lambda d: copy(LABEL, d, me).start())
     recv_emb[block(me), :] = send_emb[block(me), :]
     recv_lab[block(me), :] = send_lab[block(me), :]
 
-    others(lambda s: copy(EMB, s, s).wait_recv())
-    others(lambda s: copy(INFO, s, s).wait_recv())
-
+    side = jnp.concatenate([target_row[...], flags, jnp.zeros((6, rows), jnp.int32)], axis=0)
+    side = jnp.transpose(side.astype(jnp.float32)).astype(jnp.int32)
+    home[...] = one_hot(iota((rows, slots), 1) == side[:, 0:1])
+    kept = side[:, 1:2] > 0
+
+    whole(INFO).wait_recv()
     info = recv_info[...].reshape(n, 128).astype(jnp.bfloat16)
     slot = iota((slots, 128), 0)
     place = iota((slots, 128), 1)
@@ -151,6 +158,7 @@
     cluster_row = jnp.sum(
         jnp.where(iota((n, slots), 0) == iota((n, slots), 1) // cap, wide, 0.0), axis=0, keepdims=True
     )
+    whole(EMB).wait_recv()
     scale = 2.0 / math.sqrt(emb_ref.shape[1])
     for offset in range(0, slots, chunk):
         score = dot_nt(recv_emb[pl.ds(offset, chunk), :], recv_emb[...]) * scale
@@ -161,7 +169,7 @@
         total = jnp.sum(weight, axis=1, keepdims=True)
         affinity[pl.ds(offset, chunk), :] = (weight * (1.0 / total)).astype(jnp.bfloat16)
 
-    others(lambda s: copy(LABEL, s, s).wait_recv())
+    whole(LABEL).wait_recv()
     given = recv_lab[...].astype(jnp.float32)
     fixed = seed_col > 0.5
     carried[...] = recv_lab[...]
@@ -170,40 +178,20 @@
         current = jnp.where(fixed, given, label_mix * spread + (1.0 - label_mix) * given)
         carried[...] = current.astype(jnp.bfloat16)
 
-    def back_chunk(j, _):
+    for j in range(1, n_grp + 1):
         g = lax.rem(my_grp + j, n_grp)
         piece = pl.ds(pl.multiple_of(g * chunk, chunk), chunk)
         send_back[piece, :] = dot(affinity[piece, :], carried[...]).astype(jnp.bfloat16)
-
-        def one(k, _):
-            d = g * n_peer + lax.rem(my_peer + k, n_peer)
-
-            @pl.when(d != me)
-            def _():
-                copy(BACK, d, me).start()
-
-            return 0
-
-        lax.fori_loop(0, n_peer, one, 0)
-        return 0
-
-    lax.fori_loop(1, n_grp + 1, back_chunk, 0)
+        members_of(j, lambda d: copy(BACK, d, me).start())
     recv_back[block(me), :] = send_back[block(me), :]
 
-    side = jnp.concatenate([target_row[...], flags, jnp.zeros((6, rows), jnp.int32)], axis=0)
-    side = jnp.transpose(side.astype(jnp.float32)).astype(jnp.int32)
-    home = one_hot(iota((rows, slots), 1) == side[:, 0:1])
-    kept = side[:, 1:2] > 0
-    others(lambda s: copy(BACK, s, s).wait_recv())
-    spread = dot(home, recv_back[...])
+    whole(BACK).wait_recv()
+    spread = dot(home[...], recv_back[...])
     seed = lab_ref[...]
     out_ref[...] = jnp.where(kept, seed, label_mix * spread + (1.0 - label_mix) * seed)
 
-    def sent(d):
-        for kind in (EMB, LABEL, INFO, BACK):
-            copy(kind, d, me).wait_send()
-
-    others(sent)
+    for kind in (EMB, LABEL, INFO, BACK):
+        whole(kind).wait_send()
 
 
 def solution(mesh):
@@ -231,10 +219,11 @@
                 pltpu.VMEM((slots, width), jnp.bfloat16),
                 pltpu.VMEM((slots, width), jnp.bfloat16),
                 pltpu.VMEM((1, rows), jnp.int32),
+                pltpu.VMEM((rows, slots), jnp.bfloat16),
                 pltpu.VMEM((slots, slots), jnp.bfloat16),
                 pltpu.VMEM((slots, width), jnp.bfloat16),
-                pltpu.SemaphoreType.DMA((4, n)),
-                pltpu.SemaphoreType.DMA((4, n)),
+                pltpu.SemaphoreType.DMA((4,)),
+                pltpu.SemaphoreType.DMA((4,)),
             ],
             compiler_params=pltpu.CompilerParams(
                 collective_id=0, has_side_effects=True, vmem_limit_bytes=56 * 1024 * 1024

time: 70.9 us -> 64.3 us (0.907)
  Pallas kernels: 69 us -> 62.5 us
    pallas_call x1, Pallas kernels: 69 us -> 62.5 us  [step(): pl.pallas_call(functools.partial(kernel, n_grp, n_peer, cap), out_shape=j...]
where the time goes in v2:
time: 64.3 us; the launch traced here: 64.1 us
  Pallas kernels  62.5 us (97%)
  local copies, waits for them, and re-layouts  1.67 us (3%)
    pallas_call x1, Pallas kernels, step(): pl.pallas_call(functools.partial(kernel, n_grp, n_peer, cap), out_shape=j...  62.5 us
    unnamed x1, local copies, waits for them, and re-layouts  1.67 us

profile of v2, /device:TPU:0, one launch (start us, length us, event | category | flops | bytes accessed | tf_op | source)
XLA Modules:
  0.0 64.1 jit_solution(2213966635835132409)
XLA Ops:
  0.0 62.5 %shard_map.55 = f32[512,128]{1,0:T(8,128)} custom-call(bf16[512,768]{1,0:T(8,128)(2,1)} %emb_ref.1, f32[512,128]{1,0:T(8,128)} %lab_ref.1, s32[512]{0:T(512)} %ids_ref.1, s32[64]{0:T(128)} %own_ref.1, s32[512]{0:T(512)} %flg_ref.1), custom_call_target="tpu_custom_call" | custom-call | tf_op jit(solution)/shard_map/pallas_call | solution.py:211
  62.5 1.7 %copy.7 = f32[512,128]{1,0:T(8,128)} copy(f32[512,128]{1,0:T(8,128)} %shard_map.55) | data formatting | bytes 524288

commit v3 on v2

--- a/solution.py
+++ b/solution.py
@@ -94,7 +94,8 @@
 
     def members_of(j, body):
         g = lax.rem(my_grp + j, n_grp)
-        for k in range(1 if j == n_grp else 0, n_peer):
+        far = n_peer // 2
+        for k in sorted(range(1 if j == n_grp else 0, n_peer), key=lambda k: abs(k - far)):
             body(g * n_peer + lax.rem(my_peer + k, n_peer))
 
     barrier = pltpu.get_barrier_semaphore()
@@ -116,14 +117,6 @@
     position = jnp.sum(jnp.where(member, running, 0.0), axis=0, keepdims=True).astype(jnp.int32) - 1
     target = owner * cap + position
     target_row[...] = target
-    lane = iota((128, rows), 0)
-    entry = jnp.where(
-        lane < HALF,
-        jnp.where(lane == position, (ids + 1).astype(jnp.float32), 0.0),
-        jnp.where(lane - HALF == position, flags.astype(jnp.float32), 0.0),
-    ).astype(jnp.bfloat16)
-    send_info[...] = dot_nt(members, entry).reshape(n, 1, 128)
-    recv_info[me] = send_info[me]
 
     for j in range(1, n_grp + 1):
         g = lax.rem(my_grp + j, n_grp)
@@ -133,7 +126,16 @@
         if j == 1:
             pl.semaphore_wait(barrier, n - 1)
         members_of(j, lambda d: copy(EMB, d, me).start())
-        members_of(j, lambda d: copy(INFO, d, me).start())
+        if j == 1:
+            lane = iota((128, rows), 0)
+            entry = jnp.where(
+                lane < HALF,
+                jnp.where(lane == position, (ids + 1).astype(jnp.float32), 0.0),
+                jnp.where(lane - HALF == position, flags.astype(jnp.float32), 0.0),
+            ).astype(jnp.bfloat16)
+            send_info[...] = dot_nt(members, entry).reshape(n, 1, 128)
+            recv_info[me] = send_info[me]
+            others(lambda d: copy(INFO, d, me).start())
         send_lab[pl.ds(start, chunk), :] = dot(pick, lab_ref[...].astype(jnp.bfloat16)).astype(jnp.bfloat16)
 
     others(lambda d: copy(LABEL, d, me).start())

time: 64.3 us -> 62.6 us (0.974)
  Pallas kernels: 62.5 us -> 60.8 us
    pallas_call x1, Pallas kernels: 62.5 us -> 60.8 us  [step(): pl.pallas_call(functools.partial(kernel, n_grp, n_peer, cap), out_shape=j...]
where the time goes in v3:
time: 62.6 us; the launch traced here: 62.5 us
  Pallas kernels  60.8 us (97%)
  local copies, waits for them, and re-layouts  1.67 us (3%)
    pallas_call x1, Pallas kernels, step(): pl.pallas_call(functools.partial(kernel, n_grp, n_peer, cap), out_shape=j...  60.8 us
    unnamed x1, local copies, waits for them, and re-layouts  1.67 us

profile of v3, /device:TPU:0, one launch (start us, length us, event | category | flops | bytes accessed | tf_op | source)
XLA Modules:
  0.0 62.5 jit_solution(328021895657477763)
XLA Ops:
  0.0 60.8 %shard_map.55 = f32[512,128]{1,0:T(8,128)} custom-call(bf16[512,768]{1,0:T(8,128)(2,1)} %emb_ref.1, f32[512,128]{1,0:T(8,128)} %lab_ref.1, s32[512]{0:T(512)} %ids_ref.1, s32[64]{0:T(128)} %own_ref.1, s32[512]{0:T(512)} %flg_ref.1), custom_call_target="tpu_custom_call" | custom-call | tf_op jit(solution)/shard_map/pallas_call | solution.py:213
  60.8 1.7 %copy.7 = f32[512,128]{1,0:T(8,128)} copy(f32[512,128]{1,0:T(8,128)} %shard_map.55) | data formatting | bytes 524288

commit v4 on v3

--- a/solution.py
+++ b/solution.py
@@ -94,9 +94,12 @@
 
     def members_of(j, body):
         g = lax.rem(my_grp + j, n_grp)
-        far = n_peer // 2
-        for k in sorted(range(1 if j == n_grp else 0, n_peer), key=lambda k: abs(k - far)):
-            body(g * n_peer + lax.rem(my_peer + k, n_peer))
+        half = n_peer // 2
+        side, low = lax.div(my_peer, half), lax.rem(my_peer, half)
+        for k in range(half):
+            body(g * n_peer + (1 - side) * half + lax.rem(low + k, half))
+        for k in range(1 if j == n_grp else 0, half):
+            body(g * n_peer + side * half + lax.rem(low + k, half))
 
     barrier = pltpu.get_barrier_semaphore()
     others(

time: 62.6 us -> 63.3 us (1.011)
  Pallas kernels: 60.8 us -> 61.5 us
    pallas_call x1, Pallas kernels: 60.8 us -> 61.5 us  [step(): pl.pallas_call(functools.partial(kernel, n_grp, n_peer, cap), out_shape=j...]
where the time goes in v4:
time: 63.3 us; the launch traced here: 63.1 us
  Pallas kernels  61.5 us (97%)
  local copies, waits for them, and re-layouts  1.67 us (3%)
    pallas_call x1, Pallas kernels, step(): pl.pallas_call(functools.partial(kernel, n_grp, n_peer, cap), out_shape=j...  61.5 us
    unnamed x1, local copies, waits for them, and re-layouts  1.67 us

profile of v4, /device:TPU:0, one launch (start us, length us, event | category | flops | bytes accessed | tf_op | source)
XLA Modules:
  0.0 63.1 jit_solution(11825936992722376542)
XLA Ops:
  0.0 61.5 %shard_map.55 = f32[512,128]{1,0:T(8,128)} custom-call(bf16[512,768]{1,0:T(8,128)(2,1)} %emb_ref.1, f32[512,128]{1,0:T(8,128)} %lab_ref.1, s32[512]{0:T(512)} %ids_ref.1, s32[64]{0:T(128)} %own_ref.1, s32[512]{0:T(512)} %flg_ref.1), custom_call_target="tpu_custom_call" | custom-call | tf_op jit(solution)/shard_map/pallas_call | solution.py:216
  61.5 1.7 %copy.7 = f32[512,128]{1,0:T(8,128)} copy(f32[512,128]{1,0:T(8,128)} %shard_map.55) | data formatting | bytes 524288
